TPU v7x, 128 devices: a whole 4x4x4 slice. The times are simulated.
128 devices in a mesh: row: 16 (over z, y), col: 8 (over x, core).
Axes of the slice: x: 4, y: 4, z: 4, core: 2. Of those that a mesh axis runs over, the one named last changes fastest.
Arguments:
- inputs: bfloat16 [512, 12288], P('col', 'row'), may hold values from -6 to 6
- weight: bfloat16 [12288, 49152], P('row', 'col'), may hold values from -0.0546875 to 0.0546875
- out_grad: bfloat16 [512, 49152], P('row', 'col'), may hold values from -1.5 to 1.5
Outputs:
- output: bfloat16 [512, 49152], P('row', 'col')
- input_grad: bfloat16 [512, 12288], P('col', 'row')
- weight_grad: bfloat16 [12288, 49152], P('row', 'col')
All inputs are finite; a program needn't handle non-finite values.
Results may differ from a plain program's by a relative error of at most 0.001.
Values may be sent and summed in bfloat16 or wider, within the bound.
A program may use at most 128 MiB of HBM per device.

v0:
```python
import jax
import jax.numpy as jnp
from jax import lax
from jax.sharding import PartitionSpec as P


def shards(inputs, weight, out_grad):
    panel = lax.all_gather(inputs, "col", axis=0, tiled=True)
    output = lax.psum_scatter(
        jnp.dot(panel, weight, preferred_element_type=jnp.float32),
        "row",
        scatter_dimension=0,
        tiled=True,
    ).astype(jnp.bfloat16)
    full_grad = lax.all_gather(out_grad, "row", axis=0, tiled=True)
    input_term = lax.dot_general(
        full_grad, weight, (((1,), (1,)), ((), ())), preferred_element_type=jnp.float32
    )
    weight_total = lax.dot_general(
        panel, full_grad, (((0,), (0,)), ((), ())), preferred_element_type=jnp.float32
    )
    input_grad = lax.psum_scatter(input_term, "col", scatter_dimension=0, tiled=True).astype(
        jnp.bfloat16
    )
    return (output, input_grad, weight_total.astype(jnp.bfloat16))


def solution(mesh):
    placed = (P("col", "row"), P("row", "col"), P("row", "col"))
    return jax.shard_map(
        shards,
        mesh=mesh,
        in_specs=placed,
        out_specs=(P("row", "col"), P("col", "row"), P("row", "col")),
        check_vma=False,
    )
```

profile of v0, /device:TPU:0, one launch (start us, length us, event | category | flops | bytes accessed | tf_op | source)
XLA Modules:
  0.0 223.1 jit_solution(8867215253251750503)
XLA Ops:
  7.2 0.0 all-gather.2.cloned.1.call-start
  7.2 0.7 all-gather.2.cloned.1.call-update
  7.9 0.0 copy-start
  7.9 0.0 reduce-scatter.5.cloned.1.call-start
  8.0 66.1 %all-gather.2.cloned.1.call-done = bf16[512,6144]{1,0:T(8,128)(2,1)} async-done(((bf16[32,6144]{1,0:T(8,128)(2,1)}), bf16[512,6144]{1,0:T(8,128)(2,1)}) %all-gather.2.cloned.1.call-update) | async-done | bytes 6291472 | tf_op jit(solution)/shard_map/all_gather | solution.py:15
  74.0 10.8 %fusion.1 = f32[512,768]{1,0:T(8,128)} fusion(bf16[512,6144]{1,0:T(8,128)(2,1)} %all-gather.2.cloned.1.call-done, bf16[768,6144]{1,0:T(8,128)(2,1)} %param.4), kind=kOutput, calls=%fused_computation.2 | convolution fusion | flops 4831838208 | bytes 17301504 | tf_op jit(solution)/shard_map/dot_general | solution.py:16
  84.9 0.0 reduce-scatter.5.cloned.1.call-update
  84.9 0.0 reduce-scatter.3.cloned.1.call-start
  84.9 0.0 copy-done
  84.9 13.8 %all_gather.6 = bf16[512,768]{1,0:T(8,128)(2,1)S(1)} all-gather(bf16[64,768]{1,0:T(8,128)(2,1)S(1)} %copy-done), channel_id=1, replica_groups=mesh['row'=16,'col'=8] {'col'}, dimensions={0}, use_global_device_ids=true | all-gather | bytes 884736 | tf_op jit(solution)/shard_map/all_gather | solution.py:8
  98.7 11.7 %fusion = f32[512,6144]{1,0:T(8,128)} fusion(bf16[512,768]{1,0:T(8,128)(2,1)S(1)} %all_gather.6, bf16[768,6144]{1,0:T(8,128)(2,1)} %param.4), kind=kOutput, calls=%fused_computation.1 | convolution fusion | flops 4831838208 | bytes 22806528 | tf_op jit(solution)/shard_map/dot_general | solution.py:10
  110.4 0.0 reduce-scatter.3.cloned.1.call-update
  110.4 10.4 %convolution_convert_fusion = bf16[768,6144]{1,0:T(8,128)(2,1)} fusion(bf16[512,768]{1,0:T(8,128)(2,1)S(1)} %all_gather.6, bf16[512,6144]{1,0:T(8,128)(2,1)} %all-gather.2.cloned.1.call-done), kind=kOutput, calls=%fused_computation | convolution fusion | flops 4836556800 | bytes 16515072 | tf_op jit(solution)/shard_map/dot_general | solution.py:19
  120.8 0.0 reduce-scatter.5.cloned.1.call-done
  120.8 1.6 convert_element_type.10
  122.4 92.3 %reduce-scatter.3.cloned.1.call-done = f32[32,6144]{1,0:T(8,128)} async-done(((f32[512,6144]{1,0:T(8,128)}), f32[32,6144]{1,0:T(8,128)}) %reduce-scatter.3.cloned.1.call-update) | async-done | bytes 786448 | tf_op jit(solution)/shard_map/reduce_scatter | solution.py:9
  214.7 1.9 convert_element_type.9
Async XLA Ops:
  7.2 66.9 %all-gather.2.cloned.1.call-start = ((), (), s32[]{:S(2)}) async-start(), calls=%async_computation.3 | async-start | bytes 6684672 | tf_op jit(solution)/shard_map/all_gather | solution.py:15
  7.9 77.0 %copy-start = (bf16[64,768]{1,0:T(8,128)(2,1)S(1)}, bf16[64,768]{1,0:T(8,128)(2,1)}, u32[]{:S(2)}) copy-start(bf16[64,768]{1,0:T(8,128)(2,1)} %param.3) | copy-start | bytes 294916
  7.9 112.9 %reduce-scatter.5.cloned.1.call-start = ((), (), s32[]{:S(2)}) async-start(), calls=%async_computation.4 | async-start | bytes 1769472 | tf_op jit(solution)/shard_map/reduce_scatter | solution.py:22
  84.9 129.8 %reduce-scatter.3.cloned.1.call-start = ((), (), s32[]{:S(2)}) async-start(), calls=%async_computation.2 | async-start | bytes 13369344 | tf_op jit(solution)/shard_map/reduce_scatter | solution.py:9
Sparse Core Ops, SparseCore 0:
  10.1 63.8 all-gather.1
  85.0 32.3 reduce-scatter.4
  120.8 93.7 reduce-scatter.2
where the time goes:
time: 224 us; the launch traced here: 223 us
  waiting for transfers between devices  159 us (71%)
  matrix products  32.8 us (15%)
  blocking collectives  13.8 us (6%)
  between operations  13.8 us (6%)
  other arithmetic  3.5 us (2%)
    reduce_scatter x1, waiting for transfers between devices, shards(): lax.psum_scatter(jnp.dot(panel, weight, preferred_element_type=jnp.float3...  92.3 us
    all_gather x1, waiting for transfers between devices, shards(): full_grad = lax.all_gather(out_grad, 'row', axis=0, tiled=True)  66.1 us
    all_gather x1, blocking collectives, shards(): panel = lax.all_gather(inputs, 'col', axis=0, tiled=True)  13.8 us
    dot_general x1, matrix products, shards(): jnp.dot(panel, weight, preferred_element_type=jnp.float32)  11.7 us
    dot_general x1, matrix products, shards(): lax.dot_general(full_grad, weight, (((1,), (1,)), ((), ())), preferred_el...  10.8 us
    dot_general x1, matrix products, shards(): lax.dot_general(panel, full_grad, (((0,), (0,)), ((), ())), preferred_ele...  10.4 us
  transfers between devices with their start and end apart: 3, of which 2 were waited for; matrix products, arithmetic and copies ran while one was open for 11% of the time, Pallas kernels for 0%

commit v1 on v0

v1 whole, which is shorter than its diff:
```python
import functools

import jax
import jax.numpy as jnp
from jax import lax
from jax.experimental import pallas as pl
from jax.experimental.pallas import tpu as pltpu
from jax.sharding import PartitionSpec as P

MESH = pl.DeviceIdType.MESH
BF16 = jnp.bfloat16
F32 = jnp.float32

RING = 4
ROWS = RING * RING
CORES = 2
COLS = RING * CORES
POWER = 13
GAIN = 800.0
TINY = 1e-30

TILE = 512


def encode(v, inv):
    u = v * inv
    u2 = u * u
    u3 = u2 * u
    u6 = u3 * u3
    return (u6 * u6 * u).astype(BF16)


def decode(code, scale):
    y = code.astype(F32)
    v = jnp.exp(jnp.log(jnp.abs(y)) * (1.0 / POWER)) * scale
    return jnp.where(y < 0, -v, v)


def exchange_kernel(
    in_ref, w_ref, og_ref,
    g_out, pt_out, out_out, ig_out,
    w_v, g_v, panel, pt_v, p_v, mx_v, sc_v, snd1, rcv1, snd2, rcv2, ig_v, igr_v, igs_v, igx_v, out_v, igo_v,
    ld_sem, st_sem, ag_s, ag_r, in_s, in_r, sc_s, sc_r, r1_s, r1_r, r2_s, r2_r, co_s, co_r, xs_s, xs_r,
):
    tokens, feats = panel.shape
    quarter = g_v.shape[2]
    rb = tokens // ROWS
    cb = tokens // COLS
    tiles = quarter // TILE
    row, col = lax.axis_index("row"), lax.axis_index("col")
    z, y, x, k = row // RING, row % RING, col // CORES, col % CORES

    def ring(i, d):
        return (i + d + RING) % RING

    first, second = (y, z), (z, y)

    def row_of(h, f, g):
        return g * RING + f if h == 0 else f * RING + g

    def peer_f(h, d):
        return (row_of(h, ring(first[h], d), second[h]), col)

    def peer_g(h, d):
        return (row_of(h, first[h], ring(second[h], d)), col)

    def peer_x(d):
        return (row, ring(x, d) * CORES + k)

    partner = (row, x * CORES + (1 - k))

    def rcopy(src, dst, ss, rs, dev):
        return pltpu.make_async_remote_copy(
            src_ref=src, dst_ref=dst, send_sem=ss, recv_sem=rs, device_id=dev, device_id_type=MESH
        )

    def rows_of(r):
        return pl.ds(pl.multiple_of(r * rb, rb), rb)

    def toks_of(c):
        return pl.ds(pl.multiple_of(c * cb, cb), cb)

    g_loads = [
        pltpu.make_async_copy(og_ref.at[:, pl.ds(n * quarter, quarter)], g_v.at[n, rows_of(row)], ld_sem.at[n])
        for n in range(4)
    ]
    w_loads = [
        pltpu.make_async_copy(w_ref.at[:, pl.ds(n * quarter, quarter)], w_v.at[n], ld_sem.at[4 + n]) for n in range(4)
    ]
    in_load = pltpu.make_async_copy(in_ref, panel.at[toks_of(col)], ld_sem.at[8])
    for c in g_loads:
        c.start()
    in_load.start()
    for c in w_loads:
        c.start()

    barrier = pltpu.get_barrier_semaphore()
    peers = [peer_f(0, d) for d in (1, 2, 3)] + [peer_g(0, d) for d in (1, 2, 3)] + [peer_x(d) for d in (1, 2, 3)]
    peers.append(partner)
    for dev in peers:
        pl.semaphore_signal(barrier, inc=1, device_id=dev, device_id_type=MESH)
    pl.semaphore_wait(barrier, len(peers))

    sends = []

    def send(src, dst, ss, rs, dev):
        c = rcopy(src, dst, ss, rs, dev)
        c.start()
        sends.append(c)

    def await_recv(dst, ss, rs):
        rcopy(dst, dst, ss, rs, partner).wait_recv()

    SIGN = (1, -1)

    def g_full(h, f, g):
        return g_v.at[pl.ds(2 * h, 2), rows_of(row_of(h, f, g))]

    def g_part(h, d, f, g):
        return g_v.at[2 * h + d, rows_of(row_of(h, f, g))]

    ORDER = (0, -1, 1, 2)

    def ag1(h, d):
        ref = g_full(h, first[h], second[h])
        send(ref, ref, ag_s.at[h, d, 0], ag_r.at[h, d, 0], peer_f(h, SIGN[d]))

    def ag1_wait(h, d):
        await_recv(g_full(h, ring(first[h], -SIGN[d]), second[h]), ag_s.at[h, d, 0], ag_r.at[h, d, 0])

    def ag1f(h, d):
        ref = g_part(h, d, ring(first[h], -SIGN[d]), second[h])
        send(ref, ref, ag_s.at[h, d, 1], ag_r.at[h, d, 1], peer_f(h, SIGN[d]))

    def ag1f_wait(h, d):
        await_recv(g_part(h, d, ring(first[h], 2), second[h]), ag_s.at[h, d, 1], ag_r.at[h, d, 1])

    def ag2(h, d, j):
        ref = g_full(h, ring(first[h], ORDER[j]), second[h])
        send(ref, ref, ag_s.at[h, d, 2 + j], ag_r.at[h, d, 2 + j], peer_g(h, SIGN[d]))

    def ag2_wait(h, d, j):
        ref = g_full(h, ring(first[h], ORDER[j]), ring(second[h], -SIGN[d]))
        await_recv(ref, ag_s.at[h, d, 2 + j], ag_r.at[h, d, 2 + j])

    def ag2f(h, d, j):
        ref = g_part(h, d, ring(first[h], ORDER[j]), ring(second[h], -SIGN[d]))
        send(ref, ref, ag_s.at[h, d, 6 + j], ag_r.at[h, d, 6 + j], peer_g(h, SIGN[d]))

    def ag2f_wait(h, d, j):
        ref = g_part(h, d, ring(first[h], ORDER[j]), ring(second[h], 2))
        await_recv(ref, ag_s.at[h, d, 6 + j], ag_r.at[h, d, 6 + j])

    HD = [(h, d) for h in range(2) for d in range(2)]

    for c in g_loads:
        c.wait()
    for h, d in HD:
        ag1(h, d)
    for h, d in HD:
        ag2(h, d, 0)

    in_load.wait()
    own = panel.at[toks_of(col)]
    for d in (1, 3, 2):
        send(own, own, in_s.at[d - 1], in_r.at[d - 1], peer_x(d))
    send(own, own, in_s.at[3], in_r.at[3], partner)
    for d in (1, 3, 2):
        ref = panel.at[toks_of(ring(x, -d) * CORES + k)]
        await_recv(ref, in_s.at[d - 1], in_r.at[d - 1])
        send(ref, ref, in_s.at[3 + d], in_r.at[3 + d], partner)

    for h, d in HD:
        ag1_wait(h, d)
        ag1f(h, d)
        for e in range(2):
            ag2(h, e, 1 + d)

    for d in range(4):
        ref = panel.at[toks_of(ring(x, -d) * CORES + (1 - k))]
        await_recv(ref, in_s.at[3 + d], in_r.at[3 + d])

    mx_v[...] = jnp.zeros_like(mx_v)
    for c in w_loads:
        c.wait()

    @pl.loop(0, 4 * tiles)
    def _(i):
        n, t = i // tiles, i % tiles
        cols = pl.ds(pl.multiple_of(t * TILE, TILE), TILE)
        p = jnp.dot(panel[...], w_v[n, :, cols], preferred_element_type=F32)
        p_v[n, :, cols] = p
        mx_v[...] = jnp.maximum(mx_v[...], jnp.max(jnp.abs(p), axis=0, keepdims=True))

    sc_v[0, 0] = jnp.full(sc_v.shape[2:], jnp.max(mx_v[...]), F32)
    for d in (1, 2, 3):
        send(sc_v.at[0, 0], sc_v.at[0, d], sc_s.at[0, d - 1], sc_r.at[0, d - 1], peer_f(0, d))

    for h, d in HD:
        ag2_wait(h, d, 0)
        ag2f(h, d, 0)
    for h in range(2):
        for d in range(2):
            ag1f_wait(h, d)
        for d in range(2):
            ag2(h, d, 3)

    pt_v[...] = panel[...].T
    pt_store = pltpu.make_async_copy(pt_v, pt_out, st_sem.at[0])
    pt_store.start()

    for d in (1, 2, 3):
        await_recv(sc_v.at[0, d], sc_s.at[0, d - 1], sc_r.at[0, d - 1])
    sc_v[1, 0] = sc_v[0, 0] + sc_v[0, 1] + sc_v[0, 2] + sc_v[0, 3]
    for d in (1, 2, 3):
        send(sc_v.at[1, 0], sc_v.at[1, d], sc_s.at[1, d - 1], sc_r.at[1, d - 1], peer_g(0, d))

    for h, d in HD:
        for j in (1, 2):
            ag2_wait(h, d, j)
            ag2f(h, d, j)

    for d in (1, 2, 3):
        await_recv(sc_v.at[1, d], sc_s.at[1, d - 1], sc_r.at[1, d - 1])
    total = jnp.max(sc_v[1, 0] + sc_v[1, 1] + sc_v[1, 2] + sc_v[1, 3]) + TINY
    inv = GAIN / total
    scale = total * (1.0 / GAIN)

    def spans():
        return [pl.ds(t * TILE, TILE) for t in range(tiles)]

    def rank(j):
        return (8 - 2 - j + 3 * (j * (j - 1) // 2)) % RING

    def second_of(h, j):
        return (second[h] + rank(j)) % RING

    def r1_send(h, kind, d, j):
        rcopy(snd1.at[h, kind, d, j], rcv1.at[h, kind, d, j], r1_s.at[h, kind, d, j], r1_r.at[h, kind, d, j],
              peer_f(h, SIGN[d])).start()

    def r1_wait(h, kind, d, j):
        await_recv(rcv1.at[h, kind, d, j], r1_s.at[h, kind, d, j], r1_r.at[h, kind, d, j])

    def r2_send(h, kind, d):
        send(snd2.at[h, kind, d], rcv2.at[h, kind, d], r2_s.at[h, kind, d], r2_r.at[h, kind, d],
             peer_g(h, SIGN[d]))

    def r2_wait(h, kind, d):
        await_recv(rcv2.at[h, kind, d], r2_s.at[h, kind, d], r2_r.at[h, kind, d])

    @pl.loop(0, RING)
    def _(j):
        for h, d in HD:
            rows = rows_of(row_of(h, ring(first[h], 2), second_of(h, j)))
            for s in spans():
                snd1[h, 0, d, j, :, s] = encode(p_v[2 * h + d, rows, s], inv)
            r1_send(h, 0, d, j)

    for h, d in HD:
        ag2_wait(h, d, 3)
        ag2f(h, d, 3)

    @pl.loop(0, RING)
    def _(j):
        for h, d in HD:
            rows = rows_of(row_of(h, ring(first[h], SIGN[d]), second_of(h, j)))
            for s in spans():
                snd1[h, 1, d, j, :, s] = encode(p_v[2 * h + 1 - d, rows, s], inv)
            r1_send(h, 1, d, j)

    @pl.loop(0, RING)
    def _(j):
        for h, d in HD:
            r1_wait(h, 0, d, j)
            rows = rows_of(row_of(h, ring(first[h], SIGN[d]), second_of(h, j)))
            for s in spans():
                v = p_v[2 * h + d, rows, s] + decode(rcv1[h, 0, d, j, :, s], scale)
                snd1[h, 2, d, j, :, s] = encode(v, inv)
            r1_send(h, 2, d, j)

    for h, d in HD:
        for j in range(4):
            ag2f_wait(h, d, j)
    g_store = pltpu.make_async_copy(g_v, g_out, st_sem.at[1])
    g_store.start()

    ig_v[...] = jnp.zeros_like(ig_v)

    @pl.loop(0, 4 * tiles)
    def _(i):
        n, t = i // tiles, i % tiles
        cols = pl.ds(pl.multiple_of(t * TILE, TILE), TILE)
        term = lax.dot_general(
            g_v[n, :, cols], w_v[n, :, cols], (((1,), (1,)), ((), ())), preferred_element_type=F32
        )
        ig_v[...] += term.reshape(ig_v.shape)

    for i in range(RING):
        send(ig_v.at[i * CORES + (1 - k)], igr_v.at[i], co_s.at[i], co_r.at[i], partner)

    def fold(j):
        for h, d in HD:
            r1_wait(h, 2, d, j)
            r1_wait(h, 1, 1 - d, j)
            rows = rows_of(row_of(h, first[h], second_of(h, j)))
            for s in spans():
                p_v[2 * h + d, rows, s] = (
                    p_v[2 * h + d, rows, s]
                    + decode(rcv1[h, 2, d, j, :, s], scale)
                    + decode(rcv1[h, 1, 1 - d, j, :, s], scale)
                )

    def piece(h, q, g):
        return 2 * h + q, rows_of(row_of(h, first[h], ring(second[h], g)))

    @pl.loop(0, 1)
    def _(j):
        fold(j)

    for h, d in HD:
        n, rows = piece(h, d, 2)
        for s in spans():
            snd2[h, 0, d, :, s] = encode(p_v[n, rows, s], inv)
        r2_send(h, 0, d)

    for i in range(RING):
        await_recv(igr_v.at[i], co_s.at[i], co_r.at[i])
        igs_v[i] = ig_v[i * CORES + k] + igr_v[i]
    for d in (1, 3, 2):
        send(igs_v.at[ring(x, d)], igx_v.at[d - 1], xs_s.at[d - 1], xs_r.at[d - 1], peer_x(d))

    @pl.loop(1, 3)
    def _(j):
        fold(j)

    for h, d in HD:
        n, rows = piece(h, 1 - d, SIGN[d])
        for s in spans():
            snd2[h, 1, d, :, s] = encode(p_v[n, rows, s], inv)
        r2_send(h, 1, d)
    for h, d in HD:
        r2_wait(h, 0, d)
        n, rows = piece(h, d, SIGN[d])
        for s in spans():
            snd2[h, 2, d, :, s] = encode(p_v[n, rows, s] + decode(rcv2[h, 0, d, :, s], scale), inv)
        r2_send(h, 2, d)

    @pl.loop(3, 4)
    def _(j):
        fold(j)

    for d in (1, 3, 2):
        await_recv(igx_v.at[d - 1], xs_s.at[d - 1], xs_r.at[d - 1])
    igo_v[...] = (igs_v[x] + igx_v[0] + igx_v[1] + igx_v[2]).astype(BF16)
    ig_store = pltpu.make_async_copy(igo_v, ig_out, st_sem.at[2])
    ig_store.start()

    for h, d in HD:
        r2_wait(h, 1, 1 - d)
        r2_wait(h, 2, d)
        n, rows = piece(h, d, 0)
        for t, s in enumerate(spans()):
            v = p_v[n, rows, s] + decode(rcv2[h, 2, d, :, s], scale) + decode(rcv2[h, 1, 1 - d, :, s], scale)
            out_v[:, pl.ds(n * quarter + t * TILE, TILE)] = v.astype(BF16)
    out_store = pltpu.make_async_copy(out_v, out_out, st_sem.at[3])
    out_store.start()

    for c in sends:
        c.wait_send()

    @pl.loop(0, RING)
    def _(j):
        for h, d in HD:
            for kind in range(3):
                rcopy(snd1.at[h, kind, d, j], rcv1.at[h, kind, d, j], r1_s.at[h, kind, d, j], r1_r.at[h, kind, d, j],
                      partner).wait_send()

    for c in (pt_store, g_store, ig_store, out_store):
        c.wait()


def weight_kernel(pt_ref, g_ref, out_in, ig_in, w_out, out_out, ig_out):
    w_out[...] = jnp.dot(pt_ref[...], g_ref[0], preferred_element_type=F32).astype(BF16)

    @pl.when(pl.program_id(0) == 0)
    def _():
        out_out[...] = out_in[...]
        ig_out[...] = ig_in[...]


def shards(inputs, weight, out_grad):
    cb, feats = inputs.shape
    hidden = weight.shape[1]
    rb = out_grad.shape[0]
    tokens = rb * ROWS
    quarter = hidden // 4
    DMA = pltpu.SemaphoreType.DMA
    hbm = pl.BlockSpec(memory_space=pl.ANY)
    flops = 4 * tokens * feats * hidden
    full_grad, panel_t, output, input_grad = pl.pallas_call(
        exchange_kernel,
        out_shape=(
            jax.ShapeDtypeStruct((4, tokens, quarter), BF16),
            jax.ShapeDtypeStruct((feats, tokens), BF16),
            jax.ShapeDtypeStruct((rb, hidden), BF16),
            jax.ShapeDtypeStruct((cb, feats), BF16),
        ),
        in_specs=[hbm] * 3,
        out_specs=[hbm] * 4,
        scratch_shapes=[
            pltpu.VMEM((4, feats, quarter), BF16),
            pltpu.VMEM((4, tokens, quarter), BF16),
            pltpu.VMEM((tokens, feats), BF16),
            pltpu.VMEM((feats, tokens), BF16),
            pltpu.VMEM((4, tokens, quarter), F32),
            pltpu.VMEM((1, TILE), F32),
            pltpu.VMEM((2, RING, 8, 128), F32),
            pltpu.VMEM((2, 3, 2, RING, rb, quarter), BF16),
            pltpu.VMEM((2, 3, 2, RING, rb, quarter), BF16),
            pltpu.VMEM((2, 3, 2, rb, quarter), BF16),
            pltpu.VMEM((2, 3, 2, rb, quarter), BF16),
            pltpu.VMEM((COLS, cb, feats), F32),
            pltpu.VMEM((RING, cb, feats), F32),
            pltpu.VMEM((RING, cb, feats), F32),
            pltpu.VMEM((3, cb, feats), F32),
            pltpu.VMEM((rb, hidden), BF16),
            pltpu.VMEM((cb, feats), BF16),
            DMA((9,)),
            DMA((4,)),
            DMA((2, 2, 10)),
            DMA((2, 2, 10)),
            DMA((7,)),
            DMA((7,)),
            DMA((2, 3)),
            DMA((2, 3)),
            DMA((2, 3, 2, RING)),
            DMA((2, 3, 2, RING)),
            DMA((2, 3, 2)),
            DMA((2, 3, 2)),
            DMA((RING,)),
            DMA((RING,)),
            DMA((3,)),
            DMA((3,)),
        ],
        compiler_params=pltpu.CompilerParams(
            collective_id=0, has_side_effects=True, vmem_limit_bytes=58 * 2**20
        ),
        cost_estimate=pl.CostEstimate(flops=flops, bytes_accessed=4 * feats * hidden, transcendentals=0),
        name="exchange",
    )(inputs, weight, out_grad)

    tiles = quarter // TILE
    weight_grad, output, input_grad = pl.pallas_call(
        weight_kernel,
        grid=(4 * tiles,),
        out_shape=(
            jax.ShapeDtypeStruct((feats, hidden), BF16),
            jax.ShapeDtypeStruct((rb, hidden), BF16),
            jax.ShapeDtypeStruct((cb, feats), BF16),
        ),
        in_specs=[
            pl.BlockSpec((feats, tokens), lambda i: (0, 0)),
            pl.BlockSpec((1, tokens, TILE), lambda i: (i // tiles, 0, i % tiles)),
            pl.BlockSpec((rb, hidden), lambda i: (0, 0)),
            pl.BlockSpec((cb, feats), lambda i: (0, 0)),
        ],
        out_specs=[
            pl.BlockSpec((feats, TILE), lambda i: (0, i)),
            pl.BlockSpec((rb, hidden), lambda i: (0, 0)),
            pl.BlockSpec((cb, feats), lambda i: (0, 0)),
        ],
        compiler_params=pltpu.CompilerParams(vmem_limit_bytes=32 * 2**20),
        cost_estimate=pl.CostEstimate(
            flops=2 * tokens * feats * hidden, bytes_accessed=2 * feats * hidden, transcendentals=0
        ),
        name="weight_grad",
    )(panel_t, full_grad, output, input_grad)
    return output, input_grad, weight_grad


def solution(mesh):
    placed = (P("col", "row"), P("row", "col"), P("row", "col"))
    return jax.shard_map(
        shards,
        mesh=mesh,
        in_specs=placed,
        out_specs=(P("row", "col"), P("col", "row"), P("row", "col")),
        check_vma=False,
    )
```

time: 224 us -> 93.7 us (0.42)
  waiting for transfers between devices: 159 us -> 0 us
  Pallas kernels: 0 us -> 87 us
  matrix products: 32.8 us -> 0 us
  blocking collectives: 13.8 us -> 0 us
  between operations: 13.8 us -> 0.65 us
  local copies, waits for them, and re-layouts: 0.01 us -> 5.8 us
  other arithmetic: 3.5 us -> 0 us
    reduce_scatter x2 -> x0, waiting for transfers between devices: 92.3 us -> none  [the longest x1 92.3 us: shards(): lax.psum_scatter(jnp.dot(panel, weight, preferred_element_type=jnp.float3...]
    pallas_call x0 -> x2, Pallas kernels: none -> 87 us  [the longest x1 77.3 us: shards(): pl.pallas_call(exchange_kernel, out_shape=(jax.ShapeDtypeStruct((4, token...]
    all_gather x1 -> x0, waiting for transfers between devices: 66.1 us -> none  [shards(): full_grad = lax.all_gather(out_grad, 'row', axis=0, tiled=True)]
    dot_general x3 -> x0, matrix products: 32.8 us -> none  [the longest x1 11.7 us: shards(): jnp.dot(panel, weight, preferred_element_type=jnp.float32)]
    all_gather x1 -> x0, blocking collectives: 13.8 us -> none  [shards(): panel = lax.all_gather(inputs, 'col', axis=0, tiled=True)]
    unnamed x2 -> x8, local copies, waits for them, and re-layouts: 0.01 us -> 5.8 us
    convert_element_type x2 -> x0, other arithmetic: 3.5 us -> none  [the longest x1 1.92 us: shards(): output = lax.psum_scatter(jnp.dot(panel, weight, preferred_element_type=j...]
  transfers between devices with their start and end apart: 3 -> 0, of which waited for: 2 -> 0; matrix products, arithmetic and copies ran while one was open for 11% -> 0% of each run, Pallas kernels for 0% -> 0%
where the time goes in v1:
time: 93.7 us; the launch traced here: 93.5 us
  Pallas kernels  87 us (93%)
  local copies, waits for them, and re-layouts  5.8 us (6%)
    pallas_call x1, Pallas kernels, shards(): pl.pallas_call(exchange_kernel, out_shape=(jax.ShapeDtypeStruct((4, token...  77.3 us
    pallas_call x1, Pallas kernels, shards(): pl.pallas_call(weight_kernel, grid=(4 * tiles,), out_shape=(jax.ShapeDtyp...  9.71 us
    unnamed x8, local copies, waits for them, and re-layouts  5.8 us

profile of v1, /device:TPU:0, one launch (start us, length us, event | category | flops | bytes accessed | tf_op | source)
XLA Modules:
  0.0 93.5 jit_solution(5916723860181539511)
XLA Ops:
  0.6 77.3 %exchange.1 = (bf16[4,512,1536]{2,1,0:T(8,128)(2,1)}, bf16[768,512]{1,0:T(8,128)(2,1)}, bf16[32,6144]{1,0:T(8,128)(2,1)}, bf16[64,768]{1,0:T(8,128)(2,1)}) custom-call(bf16[64,768]{1,0:T(8,128)(2,1)} %in_ref.1, bf16[768,6144]{1,0:T(8,128)(2,1)} %w_ref.1, bf16[32,6144]{1,0:T(8,128)(2,1)} %og_ref.1), custom_call_target="tpu_custom_call" | custom-call | flops 9663676416 | bytes 18874368 | tf_op jit(solution)/shard_map/exchange/pallas_call | solution.py:401
  78.0 0.0 copy-start
  78.0 2.8 %copy-done = bf16[4,512,1536]{2,1,0:T(8,128)(2,1)S(1)} copy-done((bf16[4,512,1536]{2,1,0:T(8,128)(2,1)S(1)}, bf16[4,512,1536]{2,1,0:T(8,128)(2,1)}, u32[]{:S(2)}) %copy-start) | copy-done | bytes 6291480
  80.7 0.0 copy-start.1
  80.7 1.1 %copy-done.1 = bf16[768,512]{1,0:T(8,128)(2,1)S(1)} copy-done((bf16[768,512]{1,0:T(8,128)(2,1)S(1)}, bf16[768,512]{1,0:T(8,128)(2,1)}, u32[]{:S(2)}) %copy-start.1) | copy-done | bytes 786456
  81.9 0.0 copy-start.2
  81.9 1.0 %copy-done.2 = bf16[32,6144]{1,0:T(8,128)(2,1)S(1)} copy-done((bf16[32,6144]{1,0:T(8,128)(2,1)S(1)}, bf16[32,6144]{1,0:T(8,128)(2,1)}, u32[]{:S(2)}) %copy-start.2) | copy-done | bytes 393240
  82.9 0.0 copy-start.3
  82.9 0.9 copy-done.3
  83.8 9.7 %weight_grad.1 = (bf16[768,6144]{1,0:T(8,128)(2,1)}, bf16[32,6144]{1,0:T(8,128)(2,1)}, bf16[64,768]{1,0:T(8,128)(2,1)}) custom-call(bf16[768,512]{1,0:T(8,128)(2,1)S(1)} %copy-done.1, bf16[4,512,1536]{2,1,0:T(8,128)(2,1)S(1)} %copy-done, bf16[32,6144]{1,0:T(8,128)(2,1)S(1)} %copy-done.2, bf16[64,768]{1,0:T(8,128)(2,1)S(1)} %copy-done.3), custom_call_target="tpu_custom_call" | custom-call | flops 4831838208 | bytes 9437184 | tf_op jit(solution)/shard_map/weight_grad/pallas_call | solution.py:454
Async XLA Ops:
  78.0 2.8 %copy-start = (bf16[4,512,1536]{2,1,0:T(8,128)(2,1)S(1)}, bf16[4,512,1536]{2,1,0:T(8,128)(2,1)}, u32[]{:S(2)}) copy-start(bf16[4,512,1536]{2,1,0:T(8,128)(2,1)} %get-tuple-element.11.g_ref) | copy-start | bytes 18874372
  80.7 1.1 %copy-start.1 = (bf16[768,512]{1,0:T(8,128)(2,1)S(1)}, bf16[768,512]{1,0:T(8,128)(2,1)}, u32[]{:S(2)}) copy-start(bf16[768,512]{1,0:T(8,128)(2,1)} %get-tuple-element.10.pt_ref) | copy-start | bytes 2359300
  81.9 1.0 %copy-start.2 = (bf16[32,6144]{1,0:T(8,128)(2,1)S(1)}, bf16[32,6144]{1,0:T(8,128)(2,1)}, u32[]{:S(2)}) copy-start(bf16[32,6144]{1,0:T(8,128)(2,1)} %get-tuple-element.12.out_in) | copy-start | bytes 1179652
  82.9 0.9 copy-start.3

commit v2 on v1

--- a/solution.py
+++ b/solution.py
@@ -38,9 +38,9 @@
 
 def exchange_kernel(
     in_ref, w_ref, og_ref,
-    g_out, pt_out, out_out, ig_out,
-    w_v, g_v, panel, pt_v, p_v, mx_v, sc_v, snd1, rcv1, snd2, rcv2, ig_v, igr_v, igs_v, igx_v, out_v, igo_v,
-    ld_sem, st_sem, ag_s, ag_r, in_s, in_r, sc_s, sc_r, r1_s, r1_r, r2_s, r2_r, co_s, co_r, xs_s, xs_r,
+    wg_out, out_out, ig_out,
+    w_v, g_v, panel, pt_v, p_v, mx_v, sc_v, snd1, rcv1, snd2, rcv2, ig_v, igr_v, igs_v, igx_v,
+    ld_sem, ag_s, ag_r, in_s, in_r, sc_s, sc_r, r1_s, r1_r, r2_s, r2_r, co_s, co_r, xs_s, xs_r,
 ):
     tokens, feats = panel.shape
     quarter = g_v.shape[2]
@@ -206,8 +206,6 @@
             ag2(h, d, 3)
 
     pt_v[...] = panel[...].T
-    pt_store = pltpu.make_async_copy(pt_v, pt_out, st_sem.at[0])
-    pt_store.start()
 
     for d in (1, 2, 3):
         await_recv(sc_v.at[0, d], sc_s.at[0, d - 1], sc_r.at[0, d - 1])
@@ -282,9 +280,6 @@
     for h, d in HD:
         for j in range(4):
             ag2f_wait(h, d, j)
-    g_store = pltpu.make_async_copy(g_v, g_out, st_sem.at[1])
-    g_store.start()
-
     ig_v[...] = jnp.zeros_like(ig_v)
 
     @pl.loop(0, 4 * tiles)
@@ -314,6 +309,11 @@
     def piece(h, q, g):
         return 2 * h + q, rows_of(row_of(h, first[h], ring(second[h], g)))
 
+    def weight_quarter(n):
+        wg_out[:, pl.ds(n * quarter, quarter)] = jnp.dot(
+            pt_v[...], g_v[n], preferred_element_type=F32
+        ).astype(BF16)
+
     @pl.loop(0, 1)
     def _(j):
         fold(j)
@@ -324,12 +324,15 @@
             snd2[h, 0, d, :, s] = encode(p_v[n, rows, s], inv)
         r2_send(h, 0, d)
 
+    weight_quarter(0)
     for i in range(RING):
         await_recv(igr_v.at[i], co_s.at[i], co_r.at[i])
         igs_v[i] = ig_v[i * CORES + k] + igr_v[i]
     for d in (1, 3, 2):
         send(igs_v.at[ring(x, d)], igx_v.at[d - 1], xs_s.at[d - 1], xs_r.at[d - 1], peer_x(d))
 
+    weight_quarter(1)
+
     @pl.loop(1, 3)
     def _(j):
         fold(j)
@@ -339,6 +342,7 @@
         for s in spans():
             snd2[h, 1, d, :, s] = encode(p_v[n, rows, s], inv)
         r2_send(h, 1, d)
+    weight_quarter(2)
     for h, d in HD:
         r2_wait(h, 0, d)
         n, rows = piece(h, d, SIGN[d])
@@ -346,15 +350,15 @@
             snd2[h, 2, d, :, s] = encode(p_v[n, rows, s] + decode(rcv2[h, 0, d, :, s], scale), inv)
         r2_send(h, 2, d)
 
+    weight_quarter(3)
+
     @pl.loop(3, 4)
     def _(j):
         fold(j)
 
     for d in (1, 3, 2):
         await_recv(igx_v.at[d - 1], xs_s.at[d - 1], xs_r.at[d - 1])
-    igo_v[...] = (igs_v[x] + igx_v[0] + igx_v[1] + igx_v[2]).astype(BF16)
-    ig_store = pltpu.make_async_copy(igo_v, ig_out, st_sem.at[2])
-    ig_store.start()
+    ig_out[...] = (igs_v[x] + igx_v[0] + igx_v[1] + igx_v[2]).astype(BF16)
 
     for h, d in HD:
         r2_wait(h, 1, 1 - d)
@@ -362,9 +366,7 @@
         n, rows = piece(h, d, 0)
         for t, s in enumerate(spans()):
             v = p_v[n, rows, s] + decode(rcv2[h, 2, d, :, s], scale) + decode(rcv2[h, 1, 1 - d, :, s], scale)
-            out_v[:, pl.ds(n * quarter + t * TILE, TILE)] = v.astype(BF16)
-    out_store = pltpu.make_async_copy(out_v, out_out, st_sem.at[3])
-    out_store.start()
+            out_out[:, pl.ds(n * quarter + t * TILE, TILE)] = v.astype(BF16)
 
     for c in sends:
         c.wait_send()
@@ -376,17 +378,16 @@
                 rcopy(snd1.at[h, kind, d, j], rcv1.at[h, kind, d, j], r1_s.at[h, kind, d, j], r1_r.at[h, kind, d, j],
                       partner).wait_send()
 
-    for c in (pt_store, g_store, ig_store, out_store):
+
+def store_kernel(wg_ref, out_ref, ig_ref, wg_out, out_out, ig_out, sems):
+    copies = [
+        pltpu.make_async_copy(src, dst, sems.at[i])
+        for i, (src, dst) in enumerate(((wg_ref, wg_out), (out_ref, out_out), (ig_ref, ig_out)))
+    ]
+    for c in copies:
+        c.start()
+    for c in copies:
         c.wait()
-
-
-def weight_kernel(pt_ref, g_ref, out_in, ig_in, w_out, out_out, ig_out):
-    w_out[...] = jnp.dot(pt_ref[...], g_ref[0], preferred_element_type=F32).astype(BF16)
-
-    @pl.when(pl.program_id(0) == 0)
-    def _():
-        out_out[...] = out_in[...]
-        ig_out[...] = ig_in[...]
 
 
 def shards(inputs, weight, out_grad):
@@ -396,18 +397,14 @@
     tokens = rb * ROWS
     quarter = hidden // 4
     DMA = pltpu.SemaphoreType.DMA
-    hbm = pl.BlockSpec(memory_space=pl.ANY)
+    hbm = pl.BlockSpec(memory_space=pltpu.HBM)
     flops = 4 * tokens * feats * hidden
-    full_grad, panel_t, output, input_grad = pl.pallas_call(
+    results = (((feats, hidden), BF16), ((rb, hidden), BF16), ((cb, feats), BF16))
+    partial = pl.pallas_call(
         exchange_kernel,
-        out_shape=(
-            jax.ShapeDtypeStruct((4, tokens, quarter), BF16),
-            jax.ShapeDtypeStruct((feats, tokens), BF16),
-            jax.ShapeDtypeStruct((rb, hidden), BF16),
-            jax.ShapeDtypeStruct((cb, feats), BF16),
-        ),
+        out_shape=tuple(pltpu.VMEM(*result) for result in results),
         in_specs=[hbm] * 3,
-        out_specs=[hbm] * 4,
+        out_specs=[pl.BlockSpec(memory_space=pltpu.VMEM)] * 3,
         scratch_shapes=[
             pltpu.VMEM((4, feats, quarter), BF16),
             pltpu.VMEM((4, tokens, quarter), BF16),
@@ -424,10 +421,7 @@
             pltpu.VMEM((RING, cb, feats), F32),
             pltpu.VMEM((RING, cb, feats), F32),
             pltpu.VMEM((3, cb, feats), F32),
-            pltpu.VMEM((rb, hidden), BF16),
-            pltpu.VMEM((cb, feats), BF16),
             DMA((9,)),
-            DMA((4,)),
             DMA((2, 2, 10)),
             DMA((2, 2, 10)),
             DMA((7,)),
@@ -444,38 +438,22 @@
             DMA((3,)),
         ],
         compiler_params=pltpu.CompilerParams(
-            collective_id=0, has_side_effects=True, vmem_limit_bytes=58 * 2**20
+            collective_id=0, has_side_effects=True, vmem_limit_bytes=50 * 2**20
         ),
         cost_estimate=pl.CostEstimate(flops=flops, bytes_accessed=4 * feats * hidden, transcendentals=0),
         name="exchange",
     )(inputs, weight, out_grad)
 
-    tiles = quarter // TILE
     weight_grad, output, input_grad = pl.pallas_call(
-        weight_kernel,
-        grid=(4 * tiles,),
-        out_shape=(
-            jax.ShapeDtypeStruct((feats, hidden), BF16),
-            jax.ShapeDtypeStruct((rb, hidden), BF16),
-            jax.ShapeDtypeStruct((cb, feats), BF16),
-        ),
-        in_specs=[
-            pl.BlockSpec((feats, tokens), lambda i: (0, 0)),
-            pl.BlockSpec((1, tokens, TILE), lambda i: (i // tiles, 0, i % tiles)),
-            pl.BlockSpec((rb, hidden), lambda i: (0, 0)),
-            pl.BlockSpec((cb, feats), lambda i: (0, 0)),
-        ],
-        out_specs=[
-            pl.BlockSpec((feats, TILE), lambda i: (0, i)),
-            pl.BlockSpec((rb, hidden), lambda i: (0, 0)),
-            pl.BlockSpec((cb, feats), lambda i: (0, 0)),
-        ],
-        compiler_params=pltpu.CompilerParams(vmem_limit_bytes=32 * 2**20),
-        cost_estimate=pl.CostEstimate(
-            flops=2 * tokens * feats * hidden, bytes_accessed=2 * feats * hidden, transcendentals=0
-        ),
-        name="weight_grad",
-    )(panel_t, full_grad, output, input_grad)
+        store_kernel,
+        out_shape=tuple(jax.ShapeDtypeStruct(*result) for result in results),
+        in_specs=[pl.BlockSpec(memory_space=pltpu.VMEM)] * 3,
+        out_specs=[hbm] * 3,
+        scratch_shapes=[DMA((3,))],
+        compiler_params=pltpu.CompilerParams(vmem_limit_bytes=2 * 2**20),
+        cost_estimate=pl.CostEstimate(flops=0, bytes_accessed=2 * feats * hidden, transcendentals=0),
+        name="store",
+    )(*(p for p in partial))
     return output, input_grad, weight_grad
 
 

time: 93.7 us -> 81.4 us (0.87)
  Pallas kernels: 87 us -> 80.6 us
  local copies, waits for them, and re-layouts: 5.8 us -> 0 us
    pallas_call x2, Pallas kernels: 87 us -> 80.6 us  [the longest x1 76.7 us: shards(): pl.pallas_call(exchange_kernel, out_shape=tuple((pltpu.VMEM(*result) for...]
    unnamed x8 -> x0, local copies, waits for them, and re-layouts: 5.8 us -> none
where the time goes in v2:
time: 81.4 us; the launch traced here: 81.3 us
  Pallas kernels  80.6 us (99%)
    pallas_call x1, Pallas kernels, shards(): pl.pallas_call(exchange_kernel, out_shape=tuple((pltpu.VMEM(*result) for...  76.7 us
    pallas_call x1, Pallas kernels, shards(): pl.pallas_call(store_kernel, out_shape=tuple((jax.ShapeDtypeStruct(*resul...  3.89 us

profile of v2, /device:TPU:0, one launch (start us, length us, event | category | flops | bytes accessed | tf_op | source)
XLA Modules:
  0.0 81.3 jit_solution(1550828325549820295)
XLA Ops:
  0.6 76.7 %exchange.1 = (bf16[768,6144]{1,0:T(8,128)(2,1)S(1)}, bf16[32,6144]{1,0:T(8,128)(2,1)S(1)}, bf16[64,768]{1,0:T(8,128)(2,1)S(1)}) custom-call(bf16[64,768]{1,0:T(8,128)(2,1)} %in_ref.1, bf16[768,6144]{1,0:T(8,128)(2,1)} %w_ref.1, bf16[32,6144]{1,0:T(8,128)(2,1)} %og_ref.1), custom_call_target="tpu_custom_call" | custom-call | flops 9663676416 | bytes 18874368 | tf_op jit(solution)/shard_map/exchange/pallas_call | solution.py:403
  77.4 3.9 %store.1 = (bf16[768,6144]{1,0:T(8,128)(2,1)}, bf16[32,6144]{1,0:T(8,128)(2,1)}, bf16[64,768]{1,0:T(8,128)(2,1)}) custom-call(bf16[768,6144]{1,0:T(8,128)(2,1)S(1)} %get-tuple-element.9.wg_ref, bf16[32,6144]{1,0:T(8,128)(2,1)S(1)} %get-tuple-element.10.out_ref, bf16[64,768]{1,0:T(8,128)(2,1)S(1)} %get-tuple-element.11.ig_ref), custom_call_target="tpu_custom_call" | custom-call | bytes 9437184 | tf_op jit(solution)/shard_map/store/pallas_call | solution.py:447

commit v3 on v2

--- a/solution.py
+++ b/solution.py
@@ -80,6 +80,12 @@
     def toks_of(c):
         return pl.ds(pl.multiple_of(c * cb, cb), cb)
 
+    barrier = pltpu.get_barrier_semaphore()
+    peers = [peer_f(0, d) for d in (1, 2, 3)] + [peer_g(0, d) for d in (1, 2, 3)] + [peer_x(d) for d in (1, 2, 3)]
+    peers.append(partner)
+    for dev in peers:
+        pl.semaphore_signal(barrier, inc=1, device_id=dev, device_id_type=MESH)
+
     g_loads = [
         pltpu.make_async_copy(og_ref.at[:, pl.ds(n * quarter, quarter)], g_v.at[n, rows_of(row)], ld_sem.at[n])
         for n in range(4)
@@ -94,11 +100,6 @@
     for c in w_loads:
         c.start()
 
-    barrier = pltpu.get_barrier_semaphore()
-    peers = [peer_f(0, d) for d in (1, 2, 3)] + [peer_g(0, d) for d in (1, 2, 3)] + [peer_x(d) for d in (1, 2, 3)]
-    peers.append(partner)
-    for dev in peers:
-        pl.semaphore_signal(barrier, inc=1, device_id=dev, device_id_type=MESH)
     pl.semaphore_wait(barrier, len(peers))
 
     sends = []
@@ -259,16 +260,14 @@
         ag2_wait(h, d, 3)
         ag2f(h, d, 3)
 
-    @pl.loop(0, RING)
-    def _(j):
+    def direct(j):
         for h, d in HD:
             rows = rows_of(row_of(h, ring(first[h], SIGN[d]), second_of(h, j)))
             for s in spans():
                 snd1[h, 1, d, j, :, s] = encode(p_v[2 * h + 1 - d, rows, s], inv)
             r1_send(h, 1, d, j)
 
-    @pl.loop(0, RING)
-    def _(j):
+    def running(j):
         for h, d in HD:
             r1_wait(h, 0, d, j)
             rows = rows_of(row_of(h, ring(first[h], SIGN[d]), second_of(h, j)))
@@ -276,6 +275,11 @@
                 v = p_v[2 * h + d, rows, s] + decode(rcv1[h, 0, d, j, :, s], scale)
                 snd1[h, 2, d, j, :, s] = encode(v, inv)
             r1_send(h, 2, d, j)
+
+    @pl.loop(0, RING - 1)
+    def _(j):
+        direct(j)
+        running(j)
 
     for h, d in HD:
         for j in range(4):
@@ -324,6 +328,7 @@
             snd2[h, 0, d, :, s] = encode(p_v[n, rows, s], inv)
         r2_send(h, 0, d)
 
+    pl.loop(RING - 1, RING)(direct)
     weight_quarter(0)
     for i in range(RING):
         await_recv(igr_v.at[i], co_s.at[i], co_r.at[i])
@@ -342,6 +347,7 @@
         for s in spans():
             snd2[h, 1, d, :, s] = encode(p_v[n, rows, s], inv)
         r2_send(h, 1, d)
+    pl.loop(RING - 1, RING)(running)
     weight_quarter(2)
     for h, d in HD:
         r2_wait(h, 0, d)

time: 81.4 us -> 79.5 us (0.977)
  Pallas kernels: 80.6 us -> 78.7 us
    pallas_call x1, Pallas kernels: 76.7 us -> 74.8 us  [shards(): pl.pallas_call(exchange_kernel, out_shape=tuple((pltpu.VMEM(*result) for...]
where the time goes in v3:
time: 79.5 us; the launch traced here: 79.4 us
  Pallas kernels  78.7 us (99%)
    pallas_call x1, Pallas kernels, shards(): pl.pallas_call(exchange_kernel, out_shape=tuple((pltpu.VMEM(*result) for...  74.8 us
    pallas_call x1, Pallas kernels, shards(): pl.pallas_call(store_kernel, out_shape=tuple((jax.ShapeDtypeStruct(*resul...  3.89 us

profile of v3, /device:TPU:0, one launch (start us, length us, event | category | flops | bytes accessed | tf_op | source)
XLA Modules:
  0.0 79.4 jit_solution(16172290554750076369)
XLA Ops:
  0.6 74.8 %exchange.1 = (bf16[768,6144]{1,0:T(8,128)(2,1)S(1)}, bf16[32,6144]{1,0:T(8,128)(2,1)S(1)}, bf16[64,768]{1,0:T(8,128)(2,1)S(1)}) custom-call(bf16[64,768]{1,0:T(8,128)(2,1)} %in_ref.1, bf16[768,6144]{1,0:T(8,128)(2,1)} %w_ref.1, bf16[32,6144]{1,0:T(8,128)(2,1)} %og_ref.1), custom_call_target="tpu_custom_call" | custom-call | flops 9663676416 | bytes 18874368 | tf_op jit(solution)/shard_map/exchange/pallas_call | solution.py:409
  75.5 3.9 %store.1 = (bf16[768,6144]{1,0:T(8,128)(2,1)}, bf16[32,6144]{1,0:T(8,128)(2,1)}, bf16[64,768]{1,0:T(8,128)(2,1)}) custom-call(bf16[768,6144]{1,0:T(8,128)(2,1)S(1)} %get-tuple-element.9.wg_ref, bf16[32,6144]{1,0:T(8,128)(2,1)S(1)} %get-tuple-element.10.out_ref, bf16[64,768]{1,0:T(8,128)(2,1)S(1)} %get-tuple-element.11.ig_ref), custom_call_target="tpu_custom_call" | custom-call | bytes 9437184 | tf_op jit(solution)/shard_map/store/pallas_call | solution.py:453
